TPU v7x, 128 devices: a whole 4x4x4 slice. The times are simulated.
128 devices in a mesh: pair: 8 (over y, core), chol: 16 (over z, x).
Axes of the slice: x: 4, y: 4, z: 4, core: 2. Of those that a mesh axis runs over, the one named last changes fastest.
Arguments:
- projector: bfloat16 [8192, 4096], P('pair', 'chol'), may hold values from -6 to 6
- chol_vectors: bfloat16 [8192, 12288], P('pair', 'chol'), may hold values from -0.078125 to 0.078125
- screen_mask: int32 [64, 96], P('pair', 'chol'), may hold values 0 or 1
- amplitudes: bfloat16 [4096, 4096], P('chol', 'pair'), may hold values from -1 to 1, as said below
- pair_energy: float32 [8192], P('pair'), may hold values from 0.5 to 4
- rank_energy: float32 [4096], P('chol'), may hold values from 0.5 to 4
Outputs:
- update: float32 [8192, 4096], P('pair', 'chol')
Inputs may be any that keep to these rules, and one draw needn't show every extreme that they name: amplitudes is symmetric.
All inputs are finite; a program needn't handle non-finite values. No bound on the sum of `screen_mask` on one device may be relied on, other than what follows from the above.
Results may differ from a plain program's by a relative error of at most 0.018.
Values may be sent and summed in bfloat16 or wider, within the bound.
A program may use at most 64 MiB of HBM per device.

v0:
```python
import jax
import jax.numpy as jnp
from jax import lax
from jax.sharding import PartitionSpec as P

BLOCK = 128


def expand_mask(screen_mask):
    row_blocks, col_blocks = screen_mask.shape
    wide = jnp.broadcast_to(screen_mask[:, None, :, None], (row_blocks, BLOCK, col_blocks, BLOCK))
    return wide.reshape(row_blocks * BLOCK, col_blocks * BLOCK).astype(jnp.bfloat16)


def local(projector, chol_vectors, screen_mask, amplitudes, pair_energy, rank_energy):
    screened = chol_vectors * expand_mask(screen_mask)
    proj_full = lax.all_gather(projector, "chol", axis=1, tiled=True)
    coupling = lax.psum_scatter(
        lax.dot_general(
            proj_full, screened, (((0,), (0,)), ((), ())), preferred_element_type=jnp.float32
        ).astype(jnp.bfloat16),
        "pair",
        scatter_dimension=0,
        tiled=True,
    )
    core_cols = lax.all_gather(amplitudes, "chol", axis=0, tiled=True)
    image_rows = lax.dot_general(
        core_cols,
        lax.all_gather(coupling, "pair", axis=0, tiled=True),
        (((0,), (0,)), ((), ())),
        preferred_element_type=jnp.float32,
    ).astype(jnp.bfloat16)
    image_full = lax.all_gather(image_rows, "pair", axis=0, tiled=True)
    back_rows = lax.psum_scatter(
        lax.dot_general(
            image_full, screened, (((1,), (1,)), ((), ())), preferred_element_type=jnp.float32
        ).astype(jnp.bfloat16),
        "chol",
        scatter_dimension=0,
        tiled=True,
    ).astype(jnp.float32)
    back = back_rows.T
    return (back + projector.astype(jnp.float32)) / (pair_energy[:, None] + rank_energy[None, :])


def solution(mesh):
    placed = (
        P("pair", "chol"),
        P("pair", "chol"),
        P("pair", "chol"),
        P("chol", "pair"),
        P("pair"),
        P("chol"),
    )
    return jax.shard_map(
        local, mesh=mesh, in_specs=placed, out_specs=P("pair", "chol"), check_vma=False
    )
```

profile of v0, /device:TPU:1, one launch (start us, length us, event | category | flops | bytes accessed | tf_op | source)
XLA Modules:
  0.0 395.9 jit_solution(6470304587573010874)
XLA Ops:
  6.5 0.0 all-gather.5.cloned.1.call-start
  6.5 0.7 all-gather.5.cloned.1.call-update
  7.3 0.0 reduce-scatter.3.cloned.1.call-start
  7.3 0.7 convert_element_type.26
  8.0 0.1 copy.9
  8.1 1.7 copy.10
  9.8 80.5 %all-gather.5.cloned.1.call-done = bf16[1024,4096]{1,0:T(8,128)(2,1)} async-done(((bf16[1024,256]{1,0:T(8,128)(2,1)}), bf16[1024,4096]{1,0:T(8,128)(2,1)}) %all-gather.5.cloned.1.call-update) | async-done | bytes 8388624 | tf_op jit(solution)/shard_map/all_gather | solution.py:17
  90.3 0.3 broadcast_in_dim.2
  90.6 11.9 %fusion = bf16[4096,768]{0,1:T(8,128)(2,1)} fusion(bf16[1024,4096]{1,0:T(8,128)(2,1)} %all-gather.5.cloned.1.call-done, bf16[1024,768]{0,1:T(8,128)(2,1)S(1)} %copy.10, bf16[96,8,8,128]{3,2,1,0:T(8,128)(2,1)S(1)} %bitcast.20), kind=kOutput, calls=%fused_computation.2 | convolution fusion | flops 6446383104 | bytes 17825792 | tf_op jit(solution)/shard_map/dot_general | solution.py:19
  102.6 0.0 reduce-scatter.3.cloned.1.call-update
  102.6 0.0 all-gather.9.cloned.1.call-start
  102.6 0.7 all-gather.9.cloned.1.call-update
  103.3 0.0 all-gather.7.cloned.1.call-start
  103.4 41.4 %reduce-scatter.3.cloned.1.call-done = bf16[512,768]{0,1:T(8,128)(2,1)} async-done(((bf16[4096,768]{0,1:T(8,128)(2,1)}), bf16[512,768]{0,1:T(8,128)(2,1)}) %reduce-scatter.3.cloned.1.call-update) | async-done | bytes 786448 | tf_op jit(solution)/shard_map/reduce_scatter | solution.py:18
  144.8 0.0 all-gather.7.cloned.1.call-update
  144.8 0.0 all-gather.11.cloned.1.call-start
  144.8 54.1 %all-gather.9.cloned.1.call-done = bf16[4096,512]{1,0:T(8,128)(2,1)} async-done(((bf16[256,512]{1,0:T(8,128)(2,1)}), bf16[4096,512]{1,0:T(8,128)(2,1)}) %all-gather.9.cloned.1.call-update) | async-done | bytes 4194320 | tf_op jit(solution)/shard_map/all_gather | solution.py:26
  198.9 42.5 %all-gather.7.cloned.1.call-done = bf16[4096,768]{0,1:T(8,128)(2,1)} async-done(((bf16[512,768]{0,1:T(8,128)(2,1)}), bf16[4096,768]{0,1:T(8,128)(2,1)}) %all-gather.7.cloned.1.call-update) | async-done | bytes 6291472 | tf_op jit(solution)/shard_map/all_gather | solution.py:29
  241.4 8.3 %fusion.1 = bf16[512,768]{0,1:T(8,128)(2,1)} fusion(bf16[4096,768]{0,1:T(8,128)(2,1)} %all-gather.7.cloned.1.call-done, bf16[4096,512]{1,0:T(8,128)(2,1)} %all-gather.9.cloned.1.call-done), kind=kOutput, calls=%fused_computation.5 | convolution fusion | flops 3221618688 | bytes 11272192 | tf_op jit(solution)/shard_map/dot_general | solution.py:27
  249.7 0.0 all-gather.11.cloned.1.call-update
  249.7 0.0 reduce-scatter.5.cloned.1.call-start
  249.8 41.1 %all-gather.11.cloned.1.call-done = bf16[4096,768]{0,1:T(8,128)(2,1)} async-done(((bf16[512,768]{0,1:T(8,128)(2,1)}), bf16[4096,768]{0,1:T(8,128)(2,1)}) %all-gather.11.cloned.1.call-update) | async-done | bytes 6291472 | tf_op jit(solution)/shard_map/all_gather | solution.py:33
  290.9 12.0 %convolution_convert_fusion = bf16[4096,1024]{1,0:T(8,128)(2,1)} fusion(bf16[4096,768]{0,1:T(8,128)(2,1)} %all-gather.11.cloned.1.call-done, bf16[1024,768]{0,1:T(8,128)(2,1)S(1)} %copy.10, bf16[96,8,8,128]{3,2,1,0:T(8,128)(2,1)S(1)} %bitcast.21), kind=kOutput, calls=%fused_computation | convolution fusion | flops 6447431680 | bytes 17825792 | tf_op jit(solution)/shard_map/dot_general | solution.py:35
  302.8 0.0 copy-start
  302.8 0.0 copy-start.1
  302.9 0.0 copy-start.2
  302.9 0.0 reduce-scatter.5.cloned.1.call-update
  302.9 1.0 copy-done
  303.9 0.2 copy.11
  304.1 82.4 %reduce-scatter.5.cloned.1.call-done = bf16[256,1024]{1,0:T(8,128)(2,1)} async-done(((bf16[4096,1024]{1,0:T(8,128)(2,1)}), bf16[256,1024]{1,0:T(8,128)(2,1)}) %reduce-scatter.5.cloned.1.call-update) | async-done | bytes 524304 | tf_op jit(solution)/shard_map/reduce_scatter | solution.py:34
  386.5 0.0 copy-done.1
  386.5 0.0 copy-done.2
  386.5 1.3 fusion.2
  387.8 1.3 copy.12
Async XLA Ops:
  6.5 83.8 %all-gather.5.cloned.1.call-start = ((), (), s32[]{:S(2)}) async-start(), calls=%async_computation.2 | async-start | bytes 8912896 | tf_op jit(solution)/shard_map/all_gather | solution.py:17
  7.3 137.5 %reduce-scatter.3.cloned.1.call-start = ((), (), s32[]{:S(2)}) async-start(), calls=%async_computation.3 | async-start | bytes 7077888 | tf_op jit(solution)/shard_map/reduce_scatter | solution.py:18
  102.6 96.3 %all-gather.9.cloned.1.call-start = ((), (), s32[]{:S(2)}) async-start(), calls=%async_computation.5 | async-start | bytes 4456448 | tf_op jit(solution)/shard_map/all_gather | solution.py:26
  103.3 138.1 %all-gather.7.cloned.1.call-start = ((), (), s32[]{:S(2)}) async-start(), calls=%async_computation.4 | async-start | bytes 7077888 | tf_op jit(solution)/shard_map/all_gather | solution.py:29
  144.8 146.1 %all-gather.11.cloned.1.call-start = ((), (), s32[]{:S(2)}) async-start(), calls=%async_computation.6 | async-start | bytes 7077888 | tf_op jit(solution)/shard_map/all_gather | solution.py:33
  249.7 136.7 %reduce-scatter.5.cloned.1.call-start = ((), (), s32[]{:S(2)}) async-start(), calls=%async_computation.7 | async-start | bytes 8912896 | tf_op jit(solution)/shard_map/reduce_scatter | solution.py:34
  302.8 1.0 copy-start
  302.8 83.6 %copy-start.1 = (f32[1024]{0:T(1024)S(1)}, f32[1024]{0:T(1024)}, u32[]{:S(2)}) copy-start(f32[1024]{0:T(1024)} %param.10) | copy-start | bytes 12292
  302.9 83.6 %copy-start.2 = (f32[256]{0:T(256)S(1)}, f32[256]{0:T(256)}, u32[]{:S(2)}) copy-start(f32[256]{0:T(256)} %param.11) | copy-start | bytes 3076
Sparse Core Ops, SparseCore 0:
  9.5 80.8 all-gather.4
  102.7 42.0 reduce-scatter.2
  146.9 51.9 all-gather.8
  200.5 40.9 all-gather.6
  249.9 40.9 all-gather.10
  303.0 83.4 reduce-scatter.4
where the time goes:
time: 397 us; the launch traced here: 396 us
  waiting for transfers between devices  343 us (86%)
  matrix products  32.2 us (8%)
  between operations  13.5 us (3%)
  local copies, waits for them, and re-layouts  4.61 us (1%)
    reduce_scatter x1, waiting for transfers between devices, local(): lax.psum_scatter(lax.dot_general(image_full, screened, (((1,), (1,)), (()...  82.4 us
    all_gather x1, waiting for transfers between devices, local(): proj_full = lax.all_gather(projector, 'chol', axis=1, tiled=True)  80.5 us
    all_gather x1, waiting for transfers between devices, local(): core_cols = lax.all_gather(amplitudes, 'chol', axis=0, tiled=True)  54.1 us
    all_gather x1, waiting for transfers between devices, local(): lax.all_gather(coupling, 'pair', axis=0, tiled=True)  42.5 us
    reduce_scatter x1, waiting for transfers between devices, local(): lax.psum_scatter(lax.dot_general(proj_full, screened, (((0,), (0,)), ((),...  41.4 us
    all_gather x1, waiting for transfers between devices, local(): image_full = lax.all_gather(image_rows, 'pair', axis=0, tiled=True)  41.1 us
    dot_general x1, matrix products, local(): lax.dot_general(image_full, screened, (((1,), (1,)), ((), ())), preferred...  12 us
    dot_general x1, matrix products, local(): lax.dot_general(proj_full, screened, (((0,), (0,)), ((), ())), preferred_...  11.9 us
  transfers between devices with their start and end apart: 6, of which 6 were waited for; matrix products, arithmetic and copies ran while one was open for 1% of the time, Pallas kernels for 0%

commit v1 on v0

v1 whole, which is shorter than its diff:
```python
import jax
import jax.numpy as jnp
from jax import lax
from jax.experimental import pallas as pl
from jax.experimental.pallas import tpu as pltpu
from jax.sharding import PartitionSpec as P

MESH = pl.DeviceIdType.MESH
F32, BF16 = jnp.float32, jnp.bfloat16
TASKS = ((0, 0), (0, 1), (0, 2), (1, 0), (0, 3), (1, 1), (1, 2), (1, 3))
N_SEM = 176


def kernel(mask, p_own, s_own, a_own, out, pb, ab, xp, xr, xt, sg, tp, r1, r2, tt, bt, bp, br, fin, ss, rs):
    pair, chol = lax.axis_index("pair"), lax.axis_index("chol")
    y, k, z, x = pair // 2, pair % 2, chol // 4, chol % 4

    def at(dy=0, dz=0, dx=0, core=None, yy=None, zz=None):
        ya = (y + dy + 4) % 4 if yy is None else yy
        za = (z + dz + 4) % 4 if zz is None else zz
        ka = k if core is None else core
        return {"pair": ya * 2 + ka, "chol": za * 4 + (x + dx + 4) % 4}

    sib = at(core=1 - k)
    yl, yr, zl, zr, xl, xr_ = at(dy=-1), at(dy=1), at(dz=-1), at(dz=1), at(dx=-1), at(dx=1)
    started = []
    count = [0]

    def make(src, dst, to):
        i = count[0]
        count[0] += 1
        return pltpu.make_async_remote_copy(
            src_ref=src, dst_ref=dst, send_sem=ss.at[i], recv_sem=rs.at[i], device_id=to, device_id_type=MESH
        )

    def send(src, dst, to):
        copy = make(src, dst, to)
        copy.start()
        started.append(copy)
        return copy

    barrier = pltpu.get_barrier_semaphore()
    friends = [sib, yl, yr, zl, zr, xl, xr_, at(dx=2), at(dy=2), at(dz=2), at(yy=z, zz=y, core=1 - k)]
    for friend in friends:
        pl.semaphore_signal(barrier, inc=1, device_id=friend, device_id_type=MESH)
    off = y != z

    @pl.when(off)
    def _():
        pl.semaphore_signal(barrier, inc=1, device_id=at(yy=z, zz=y), device_id_type=MESH)

    krow = pl.multiple_of(k * 1024, 1024)
    for i in range(8):
        rows = pl.ds(pl.multiple_of(krow + i * 128, 128), 128)
        for j in range(6):
            keep = mask[i, j].astype(F32)
            block = s_own[i * 128 : (i + 1) * 128, j * 128 : (j + 1) * 128].astype(F32) * keep
            sg[0, rows, j * 128 : (j + 1) * 128] = block.astype(BF16)
    zcol = pl.ds(pl.multiple_of(z * 256, 256), 256)
    krows = pl.ds(krow, 1024)
    half = [pl.ds(pl.multiple_of(krow + u * 512, 512), 512) for u in range(2)]
    pb[krows, zcol] = p_own[...]

    @pl.when(off)
    def _():
        pl.semaphore_wait(barrier, 12)

    @pl.when(y == z)
    def _():
        pl.semaphore_wait(barrier, 11)

    p_r0 = send(p_own.at[:512], pb.at[half[0], zcol], zr)
    p_l1 = send(p_own.at[512:], pb.at[half[1], zcol], zl)
    krows_a = pl.ds(pl.multiple_of(k * 128, 128), 128)
    a_dst = ab.at[:, krows_a, zcol]
    a_other = send(a_own.at[1 - k], a_dst, at(yy=z, zz=y, core=1 - k))
    a_same = make(a_own.at[k], a_dst, at(yy=z, zz=y))

    @pl.when(off)
    def _():
        a_same.start()

    @pl.when(y == z)
    def _():
        ab[:, krows_a, zcol] = a_own[k]

    p_r1 = send(p_own.at[512:], pb.at[half[1], zcol], zr)
    p_l0 = send(p_own.at[:512], pb.at[half[0], zcol], zl)
    p_sib = send(p_own, pb.at[krows, zcol], sib)
    lo, hi = slice(0, 384), slice(384, 768)
    own_lo, own_hi = sg.at[0, krows, lo], sg.at[0, krows, hi]
    s_r0 = send(own_lo, sg.at[1, krows, hi], xr_)
    s_l0 = send(own_lo, sg.at[1, krows, lo], xl)
    s_sib = send(sg.at[0, krows], sg.at[0, krows], sib)

    a_other.wait_recv()

    @pl.when(off)
    def _():
        a_same.wait_recv()

    ycol = pl.ds(pl.multiple_of(y * 256, 256), 256)
    a_all = [send(ab.at[:, :, ycol], ab.at[:, :, ycol], at(dy=d)) for d in (1, 3, 2)]

    def col(d):
        return pl.ds(pl.multiple_of((z + d + 4) % 4 * 256, 256), 256)

    def share(ref):
        return send(ref, ref, sib)

    shares = [p_sib]
    p_r0.wait_recv()
    ref = pb.at[half[0], col(-1)]
    p_fr = send(ref, ref, zr)
    shares.append(share(ref))
    p_l1.wait_recv()
    ref = pb.at[half[1], col(1)]
    p_fl = send(ref, ref, zl)
    shares.append(share(ref))
    p_r1.wait_recv()
    shares.append(share(pb.at[half[1], col(-1)]))
    p_l0.wait_recv()
    shares.append(share(pb.at[half[0], col(1)]))
    p_fr.wait_recv()
    shares.append(share(pb.at[half[0], col(2)]))
    p_fl.wait_recv()
    shares.append(share(pb.at[half[1], col(2)]))
    for copy in a_all + shares:
        copy.wait_recv()

    x_parts = []
    for h in range(2):
        part = lax.dot_general(ab[h], pb[...], (((1,), (1,)), ((), ())), preferred_element_type=F32)
        xp[h] = part.astype(BF16).reshape(4, 64, 2048)
        x_parts.append([send(xp.at[h, (x + d) % 4], xr.at[h, d - 1], at(dx=d)) for d in (1, 3, 2)])
    s_r1 = send(own_hi, sg.at[2, krows, hi], xr_)
    s_l1 = send(own_hi, sg.at[2, krows, lo], xl)
    zrow = pl.ds(pl.multiple_of(z * 64, 64), 64)
    x_all = []
    for h in range(2):
        for copy in x_parts[h]:
            copy.wait_recv()
        total = xp[h, x].astype(F32)
        for d in range(3):
            total += xr[h, d].astype(F32)
        xt[h, zrow, :] = total.astype(BF16)
        x_all.append([send(xt.at[h, zrow], xt.at[h, zrow], at(dz=d)) for d in (1, 3, 2)])

    s_sib.wait_recv()
    s_r0.wait_recv()
    s_fr = send(sg.at[1, krows, hi], sg.at[3, krows, lo], xr_)
    g1 = [share(sg.at[1, krows, hi])]
    s_l0.wait_recv()
    g1.append(share(sg.at[1, krows, lo]))

    def ready(g):
        if g == 1:
            for copy in g1:
                copy.wait_recv()
        if g == 2:
            s_r1.wait_recv()
            shared = [share(sg.at[2, krows, hi])]
            s_l1.wait_recv()
            s_fl[0] = send(sg.at[2, krows, lo], sg.at[3, krows, hi], xl)
            shared.append(share(sg.at[2, krows, lo]))
            for copy in shared:
                copy.wait_recv()
        if g == 3:
            s_fr.wait_recv()
            shared = [share(sg.at[3, krows, lo])]
            s_fl[0].wait_recv()
            shared.append(share(sg.at[3, krows, hi]))
            for copy in shared:
                copy.wait_recv()

    s_fl = [None]
    up, down, opp = (y + 1) % 4, (y + 3) % 4, (y + 2) % 4
    first, second = slice(0, 32), slice(32, 64)
    state = [{} for _ in TASKS]
    have_x, have_s = set(), {0}

    def stage0(t):
        h, g = TASKS[t]
        if h not in have_x:
            have_x.add(h)
            for copy in x_all[h]:
                copy.wait_recv()
        if g not in have_s:
            have_s.add(g)
            ready(g)
        part = jnp.dot(xt[h], sg[g], preferred_element_type=F32)
        tp[t] = part.astype(BF16).reshape(4, 64, 768)
        s = state[t]
        s["a"] = send(tp.at[t, opp, first], r1.at[t, 0], yr)
        s["b"] = send(tp.at[t, opp, second], r1.at[t, 1], yl)
        s["c"] = send(tp.at[t, up, second], r2.at[t, 0, second], yr)
        s["d"] = send(tp.at[t, down, first], r2.at[t, 1, first], yl)

    def stage1(t):
        s = state[t]
        s["a"].wait_recv()
        tp[t, up, first, :] = (tp[t, up, first, :].astype(F32) + r1[t, 0].astype(F32)).astype(BF16)
        s["e"] = send(tp.at[t, up, first], r2.at[t, 0, first], yr)
        s["b"].wait_recv()
        tp[t, down, second, :] = (tp[t, down, second, :].astype(F32) + r1[t, 1].astype(F32)).astype(BF16)
        s["f"] = send(tp.at[t, down, second], r2.at[t, 1, second], yl)

    def rows_of(index, start=0, size=64):
        return pl.ds(pl.multiple_of(index * 64 + start, 32), size)

    def stage2(t):
        h, g = TASKS[t]
        s = state[t]
        for name in "cdef":
            s[name].wait_recv()
        total = tp[t, y].astype(F32) + r2[t, 0].astype(F32) + r2[t, 1].astype(F32)
        mine = tt.at[h, g, rows_of(y)]
        tt[h, g, rows_of(y), :] = total.astype(BF16)
        s["g"] = send(mine, mine, yr)
        s["h"] = send(mine, mine, yl)

    def stage3(t):
        h, g = TASKS[t]
        s = state[t]
        s["g"].wait_recv()
        ref = tt.at[h, g, rows_of(down, 0, 32)]
        s["i"] = send(ref, ref, yr)
        s["h"].wait_recv()
        ref = tt.at[h, g, rows_of(up, 32, 32)]
        s["j"] = send(ref, ref, yl)

    done = [0, 0]
    b_parts = [None, None]

    def stage4(t):
        h, g = TASKS[t]
        s = state[t]
        s["i"].wait_recv()
        s["j"].wait_recv()
        part = lax.dot_general(tt[h, g], sg[g], (((1,), (1,)), ((), ())), preferred_element_type=F32)
        if done[h]:
            part += bt[h]
        done[h] += 1
        bt[h] = part
        if done[h] == 4:
            bp[h] = part.astype(BF16).reshape(4, 64, 2048)
            b_parts[h] = [send(bp.at[h, (z + d) % 4], br.at[h, d - 1], at(dz=d)) for d in (2, 1, 3)]

    stages = (stage0, stage1, stage2, stage3, stage4)
    for tick in range(len(TASKS) + 4):
        for back in (4, 3, 2, 1, 0):
            if 0 <= tick - back < len(TASKS):
                stages[back](tick - back)

    other = pl.ds(pl.multiple_of((1 - k) * 1024, 1024), 1024)
    finals = []
    for h in range(2):
        for copy in b_parts[h]:
            copy.wait_recv()
        total = bt[h, zrow, :]
        for d in range(3):
            total += br[h, d].astype(F32)
        bt[h, zrow, :] = total
        finals.append(send(bt.at[h, zrow, other], fin.at[h], sib))
        out[pl.ds(pl.multiple_of(k * 128 + h * 64, 64), 64), :] = bt[h, zrow, krows]
    for h in range(2):
        finals[h].wait_recv()
        out[pl.ds(pl.multiple_of((1 - k) * 128 + h * 64, 64), 64), :] = fin[h]
    for copy in started:
        copy.wait_send()

    @pl.when(off)
    def _():
        a_same.wait_send()


def local(projector, chol_vectors, screen_mask, amplitudes, pair_energy, rank_energy):
    a_own = amplitudes.T.reshape(2, 2, 2, 64, 256).transpose(1, 2, 0, 3, 4).reshape(2, 2, 128, 256)
    vmem = pl.BlockSpec(memory_space=pltpu.VMEM)
    back = pl.pallas_call(
        kernel,
        out_shape=jax.ShapeDtypeStruct((256, 1024), F32),
        in_specs=[pl.BlockSpec(memory_space=pltpu.SMEM), vmem, vmem, vmem],
        out_specs=vmem,
        scratch_shapes=[
            pltpu.VMEM((2048, 1024), BF16),
            pltpu.VMEM((2, 256, 1024), BF16),
            pltpu.VMEM((2, 4, 64, 2048), BF16),
            pltpu.VMEM((2, 3, 64, 2048), BF16),
            pltpu.VMEM((2, 256, 2048), BF16),
            pltpu.VMEM((4, 2048, 768), BF16),
            pltpu.VMEM((8, 4, 64, 768), BF16),
            pltpu.VMEM((8, 2, 32, 768), BF16),
            pltpu.VMEM((8, 2, 64, 768), BF16),
            pltpu.VMEM((2, 4, 256, 768), BF16),
            pltpu.VMEM((2, 256, 2048), F32),
            pltpu.VMEM((2, 4, 64, 2048), BF16),
            pltpu.VMEM((2, 3, 64, 2048), BF16),
            pltpu.VMEM((2, 64, 1024), F32),
            pltpu.SemaphoreType.DMA((N_SEM,)),
            pltpu.SemaphoreType.DMA((N_SEM,)),
        ],
        compiler_params=pltpu.CompilerParams(
            collective_id=0, has_side_effects=True, vmem_limit_bytes=58 * 1024 * 1024
        ),
        cost_estimate=pl.CostEstimate(flops=16 * 10**9, bytes_accessed=8 * 10**6, transcendentals=0),
    )(screen_mask, projector, chol_vectors, a_own)
    return (back.T + projector.astype(F32)) / (pair_energy[:, None] + rank_energy[None, :])


def solution(mesh):
    placed = (
        P("pair", "chol"),
        P("pair", "chol"),
        P("pair", "chol"),
        P("chol", "pair"),
        P("pair"),
        P("chol"),
    )
    return jax.shard_map(local, mesh=mesh, in_specs=placed, out_specs=P("pair", "chol"), check_vma=False)
```

time: 397 us -> 166 us (0.42)
  waiting for transfers between devices: 343 us -> 0 us
  Pallas kernels: 0 us -> 160 us
  matrix products: 32.2 us -> 0 us
  between operations: 13.5 us -> 0.06 us
    all_gather x4 -> x0, waiting for transfers between devices: 218 us -> none  [the longest x1 80.5 us: local(): proj_full = lax.all_gather(projector, 'chol', axis=1, tiled=True)]
    pallas_call x0 -> x1, Pallas kernels: none -> 160 us  [local(): pl.pallas_call(kernel, out_shape=jax.ShapeDtypeStruct((256, 1024), F32),...]
    reduce_scatter x2 -> x0, waiting for transfers between devices: 124 us -> none  [the longest x1 82.4 us: local(): lax.psum_scatter(lax.dot_general(image_full, screened, (((1,), (1,)), (()...]
    dot_general x3 -> x0, matrix products: 32.2 us -> none  [the longest x1 12 us: local(): lax.dot_general(image_full, screened, (((1,), (1,)), ((), ())), preferred...]
  transfers between devices with their start and end apart: 6 -> 0, of which waited for: 6 -> 0; matrix products, arithmetic and copies ran while one was open for 1% -> 0% of each run, Pallas kernels for 0% -> 0%
where the time goes in v1:
time: 166 us
  Pallas kernels  160 us (96%)
  local copies, waits for them, and re-layouts  4.37 us (3%)
    pallas_call x1, Pallas kernels, local(): pl.pallas_call(kernel, out_shape=jax.ShapeDtypeStruct((256, 1024), F32),...  160 us

profile of v1, /device:TPU:1, one launch (start us, length us, event | category | flops | bytes accessed | tf_op | source)
XLA Modules:
  0.0 165.7 jit_solution(4261296055592163849)
XLA Ops:
  0.0 1.1 copy.10
  1.1 0.7 copy.11
  1.8 1.2 copy.12
  3.1 0.0 copy-start
  3.1 0.0 copy-start.1
  3.1 159.8 %shard_map.64 = f32[256,1024]{1,0:T(8,128)} custom-call(s32[8,6]{1,0:T(8,128)} %mask.1, bf16[1024,256]{1,0:T(8,128)(2,1)} %p_own.1, bf16[1024,768]{1,0:T(8,128)(2,1)} %s_own.1, bf16[2,2,128,256]{3,2,1,0:T(8,128)(2,1)} %bitcast.11), custom_call_target="tpu_custom_call" | custom-call | flops 16000000000 | bytes 8000000 | tf_op jit(solution)/shard_map/pallas_call | solution.py:280
  162.9 0.0 copy-done
  162.9 0.0 copy-done.1
  162.9 1.5 fusion
  164.4 1.3 copy.13
Async XLA Ops:
  3.1 159.8 %copy-start = (f32[1024]{0:T(1024)S(1)}, f32[1024]{0:T(1024)}, u32[]{:S(2)}) copy-start(f32[1024]{0:T(1024)} %param.10) | copy-start | bytes 12292
  3.1 159.8 %copy-start.1 = (f32[256]{0:T(256)S(1)}, f32[256]{0:T(256)}, u32[]{:S(2)}) copy-start(f32[256]{0:T(256)} %param.11) | copy-start | bytes 3076

commit v2 on v1

v2 whole, which is shorter than its diff:
```python
import jax
import jax.numpy as jnp
from jax import lax
from jax.experimental import pallas as pl
from jax.experimental.pallas import tpu as pltpu
from jax.sharding import PartitionSpec as P

MESH = pl.DeviceIdType.MESH
F32, BF16 = jnp.float32, jnp.bfloat16
TASKS = ((0, 0), (0, 1), (1, 0), (1, 1), (0, 2), (1, 2), (0, 3), (1, 3))
N_SEM = 200


def kernel(mask, p_own, s_own, a_own, out, pb, ab, xp, xr, xt, sg, tp, r1, r2, tt, bt, bp, br, fin, ss, rs):
    pair, chol = lax.axis_index("pair"), lax.axis_index("chol")
    y, k, z, x = pair // 2, pair % 2, chol // 4, chol % 4

    def at(dy=0, dz=0, dx=0, core=None, yy=None, zz=None):
        ya = (y + dy + 4) % 4 if yy is None else yy
        za = (z + dz + 4) % 4 if zz is None else zz
        ka = k if core is None else core
        return {"pair": ya * 2 + ka, "chol": za * 4 + (x + dx + 4) % 4}

    sib = at(core=1 - k)
    yl, yr, zl, zr, xl, xr_ = at(dy=-1), at(dy=1), at(dz=-1), at(dz=1), at(dx=-1), at(dx=1)
    started = []
    count = [0]

    def make(src, dst, to):
        i = count[0]
        count[0] += 1
        return pltpu.make_async_remote_copy(
            src_ref=src, dst_ref=dst, send_sem=ss.at[i], recv_sem=rs.at[i], device_id=to, device_id_type=MESH
        )

    def send(src, dst, to):
        copy = make(src, dst, to)
        copy.start()
        started.append(copy)
        return copy

    barrier = pltpu.get_barrier_semaphore()
    friends = [sib, yl, yr, zl, zr, xl, xr_, at(dx=2), at(dy=2), at(dz=2)] + [at(dx=d, core=1 - k) for d in (1, 2, 3)]
    for friend in friends:
        pl.semaphore_signal(barrier, inc=1, device_id=friend, device_id_type=MESH)
    for i in range(8):
        u, rows = i // 4, slice(i % 4 * 128, i % 4 * 128 + 128)
        for j in range(6):
            keep = mask[i, j].astype(F32)
            block = s_own[i * 128 : (i + 1) * 128, j * 128 : (j + 1) * 128].astype(F32) * keep
            sg[0, u, k, rows, j * 128 : (j + 1) * 128] = block.astype(BF16)
    zcol = pl.ds(pl.multiple_of(z * 256, 256), 256)
    for u in range(2):
        pb[u, k, :, zcol] = p_own[u * 512 : (u + 1) * 512]
    pl.semaphore_wait(barrier, len(friends))

    ycol = pl.ds(pl.multiple_of(y * 256, 256), 256)
    a_rows = pl.ds(pl.multiple_of(x * 64, 64), 64)
    a_first = count[0]
    count[0] += 4
    a_sends = []
    for j in range(2):
        for core in range(2):
            copy = pltpu.make_async_remote_copy(
                src_ref=a_own.at[core, :, :, j * 256 : (j + 1) * 256],
                dst_ref=ab.at[:, a_rows, ycol],
                send_sem=ss.at[a_first + j * 2 + core],
                recv_sem=rs.at[a_first + x],
                device_id={"pair": y * 2 + core, "chol": z * 4 + 2 * k + j},
                device_id_type=MESH,
            )
            away = jnp.logical_or(2 * k + j != x, k != core)
            a_sends.append((away, copy))

            @pl.when(away)
            def _():
                copy.start()

            @pl.when(jnp.logical_not(away))
            def _():
                ab[:, a_rows, ycol] = a_own[core, :, :, j * 256 : (j + 1) * 256]

    a256, b256 = slice(0, 256), slice(256, 512)
    p_r0 = send(pb.at[0, k, :, zcol], pb.at[0, k, :, zcol], zr)
    p_l0 = send(pb.at[0, k, :, zcol], pb.at[0, k, :, zcol], zl)
    p_ra = send(pb.at[1, k, a256, zcol], pb.at[1, k, a256, zcol], zr)
    p_lb = send(pb.at[1, k, b256, zcol], pb.at[1, k, b256, zcol], zl)
    p_sib = send(pb.at[:, k, :, zcol], pb.at[:, k, :, zcol], sib)
    lo, hi = slice(0, 384), slice(384, 768)
    s_r0 = [send(sg.at[0, u, k, :, lo], sg.at[1, u, k, :, hi], xr_) for u in range(2)]
    s_l0 = [send(sg.at[0, u, k, :, lo], sg.at[1, u, k, :, lo], xl) for u in range(2)]
    s_sib = send(sg.at[0, :, k], sg.at[0, :, k], sib)

    for source in range(4):

        @pl.when(jnp.logical_or(source != x, x // 2 != k))
        def _():
            pltpu.make_async_remote_copy(
                src_ref=ab.at[:, a_rows, ycol],
                dst_ref=ab.at[:, source * 64 : (source + 1) * 64, ycol],
                send_sem=ss.at[a_first],
                recv_sem=rs.at[a_first + source],
                device_id=xr_,
                device_id_type=MESH,
            ).wait_recv()

    a_all = [[send(ab.at[h, :, ycol], ab.at[h, :, ycol], at(dy=d)) for d in (1, 3, 2)] for h in range(2)]

    def col(d):
        return pl.ds(pl.multiple_of((z + d + 4) % 4 * 256, 256), 256)

    def share(ref):
        return send(ref, ref, sib)

    units = ((0, 0), (0, 1), (1, 0), (1, 1))
    x_parts = []

    def x_unit(h, u):
        part = lax.dot_general(
            ab[h], pb[u].reshape(1024, 1024), (((1,), (1,)), ((), ())), preferred_element_type=F32
        )
        xp[h, u] = part.astype(BF16).reshape(4, 64, 1024)
        x_parts.append([send(xp.at[h, u, (x + d) % 4], xr.at[h, u, d - 1], at(dx=d)) for d in (2, 1, 3)])

    p_r0.wait_recv()
    ref = pb.at[0, k, a256, col(-1)]
    p_fr0 = send(ref, ref, zr)
    p_l0.wait_recv()
    ref = pb.at[0, k, b256, col(1)]
    p_fl0 = send(ref, ref, zl)
    p_rb = send(pb.at[1, k, b256, zcol], pb.at[1, k, b256, zcol], zr)
    p_la = send(pb.at[1, k, a256, zcol], pb.at[1, k, a256, zcol], zl)
    shares = [p_sib, share(pb.at[0, k, :, col(-1)]), share(pb.at[0, k, :, col(1)])]
    p_ra.wait_recv()
    ref = pb.at[1, k, a256, col(-1)]
    p_fr1 = send(ref, ref, zr)
    shares1 = [share(ref)]
    p_fr0.wait_recv()
    shares.append(share(pb.at[0, k, a256, col(2)]))
    p_fl0.wait_recv()
    shares.append(share(pb.at[0, k, b256, col(2)]))
    p_lb.wait_recv()
    ref = pb.at[1, k, b256, col(1)]
    p_fl1 = send(ref, ref, zl)
    shares1.append(share(ref))
    for copy in a_all[0] + shares:
        copy.wait_recv()

    x_unit(0, 0)
    p_rb.wait_recv()
    shares1.append(share(pb.at[1, k, b256, col(-1)]))
    p_la.wait_recv()
    shares1.append(share(pb.at[1, k, a256, col(1)]))
    p_fr1.wait_recv()
    shares1.append(share(pb.at[1, k, a256, col(2)]))
    p_fl1.wait_recv()
    shares1.append(share(pb.at[1, k, b256, col(2)]))
    for copy in shares1:
        copy.wait_recv()
    x_unit(0, 1)
    for copy in a_all[1]:
        copy.wait_recv()
    x_unit(1, 0)
    x_unit(1, 1)
    s_r1 = [send(sg.at[0, u, k, :, hi], sg.at[2, u, k, :, hi], xr_) for u in range(2)]
    s_l1 = [send(sg.at[0, u, k, :, hi], sg.at[2, u, k, :, lo], xl) for u in range(2)]

    s_shares = [None, [], [], []]
    s_fr, s_fl = [], []
    for u in range(2):
        s_r0[u].wait_recv()
        s_fr.append(send(sg.at[1, u, k, :, hi], sg.at[3, u, k, :, lo], xr_))
        s_l0[u].wait_recv()
        s_shares[1].append(share(sg.at[1, u, k]))

    zrow = pl.ds(pl.multiple_of(z * 64, 64), 64)
    x_all = [[], []]

    def x_sum(h, u):
        for copy in x_parts[h * 2 + u]:
            copy.wait_recv()
        total = xp[h, u, x].astype(F32)
        for d in range(3):
            total += xr[h, u, d].astype(F32)
        mine = xt.at[h, zrow, u * 1024 : (u + 1) * 1024]
        xt[h, zrow, u * 1024 : (u + 1) * 1024] = total.astype(BF16)
        x_all[h].extend([send(mine, mine, at(dz=d)) for d in (2, 1, 3)])

    x_sum(0, 0)
    x_sum(0, 1)
    s_sib.wait_recv()
    x_sum(1, 0)

    def far(u):
        s_r1[u].wait_recv()
        s_l1[u].wait_recv()
        s_fl.append(send(sg.at[2, u, k, :, lo], sg.at[3, u, k, :, hi], xl))
        s_shares[2].append(share(sg.at[2, u, k]))

    def farther(u):
        s_fr[u].wait_recv()
        s_fl[u].wait_recv()
        s_shares[3].append(share(sg.at[3, u, k]))

    after = {0: (lambda: x_sum(1, 1),), 2: (lambda: far(0),), 3: (lambda: far(1),), 5: (lambda: farther(0), lambda: farther(1))}

    up, down, opp = (y + 1) % 4, (y + 3) % 4, (y + 2) % 4
    first, second = slice(0, 32), slice(32, 64)
    state = [{} for _ in TASKS]
    have_x, have_s = set(), {0}

    def stage0(t):
        h, g = TASKS[t]
        if h not in have_x:
            have_x.add(h)
            for copy in x_all[h]:
                copy.wait_recv()
        if g not in have_s:
            have_s.add(g)
            for copy in s_shares[g]:
                copy.wait_recv()
        part = jnp.dot(xt[h], sg[g].reshape(2048, 768), preferred_element_type=F32)
        tp[t] = part.astype(BF16).reshape(4, 64, 768)
        s = state[t]
        s["a"] = send(tp.at[t, opp, first], r1.at[t, 0], yr)
        s["b"] = send(tp.at[t, opp, second], r1.at[t, 1], yl)
        s["c"] = send(tp.at[t, up, second], r2.at[t, 0, second], yr)
        s["d"] = send(tp.at[t, down, first], r2.at[t, 1, first], yl)

    def stage1(t):
        s = state[t]
        s["a"].wait_recv()
        tp[t, up, first, :] = (tp[t, up, first, :].astype(F32) + r1[t, 0].astype(F32)).astype(BF16)
        s["e"] = send(tp.at[t, up, first], r2.at[t, 0, first], yr)
        s["b"].wait_recv()
        tp[t, down, second, :] = (tp[t, down, second, :].astype(F32) + r1[t, 1].astype(F32)).astype(BF16)
        s["f"] = send(tp.at[t, down, second], r2.at[t, 1, second], yl)

    def rows_of(index, start=0, size=64):
        return pl.ds(pl.multiple_of(index * 64 + start, 32), size)

    def stage2(t):
        h, g = TASKS[t]
        s = state[t]
        for name in "cdef":
            s[name].wait_recv()
        total = tp[t, y].astype(F32) + r2[t, 0].astype(F32) + r2[t, 1].astype(F32)
        mine = tt.at[h, g, rows_of(y)]
        tt[h, g, rows_of(y), :] = total.astype(BF16)
        s["g"] = send(mine, mine, yr)
        s["h"] = send(mine, mine, yl)

    def stage3(t):
        h, g = TASKS[t]
        s = state[t]
        s["g"].wait_recv()
        ref = tt.at[h, g, rows_of(down, 0, 32)]
        s["i"] = send(ref, ref, yr)
        s["h"].wait_recv()
        ref = tt.at[h, g, rows_of(up, 32, 32)]
        s["j"] = send(ref, ref, yl)

    done = [0, 0]
    b_parts = [None, None]

    def stage4(t):
        h, g = TASKS[t]
        s = state[t]
        s["i"].wait_recv()
        s["j"].wait_recv()
        part = lax.dot_general(tt[h, g], sg[g].reshape(2048, 768), (((1,), (1,)), ((), ())), preferred_element_type=F32)
        if done[h]:
            part += bt[h]
        done[h] += 1
        bt[h] = part
        if done[h] == 4:
            bp[h] = part.astype(BF16).reshape(4, 64, 2048)
            b_parts[h] = [send(bp.at[h, (z + d) % 4], br.at[h, d - 1], at(dz=d)) for d in (2, 1, 3)]

    stages = (stage0, stage1, stage2, stage3, stage4)
    for tick in range(len(TASKS) + 4):
        for back in (4, 3, 2, 1, 0):
            if 0 <= tick - back < len(TASKS):
                stages[back](tick - back)
        for step in after.get(tick, ()):
            step()


    def q_cols(u, core):
        return pl.ds(pl.multiple_of(u * 1024 + core * 512, 512), 512)

    finals = []

    def fin_rows(core, h):
        return pl.ds(pl.multiple_of(core * 128 + h * 64, 64), 64)

    for h in range(2):
        for copy in b_parts[h]:
            copy.wait_recv()
        total = bt[h, zrow, :]
        for d in range(3):
            total += br[h, d].astype(F32)
        bt[h, zrow, :] = total
        for u in range(2):
            cols = slice(u * 512, u * 512 + 512)
            finals.append(send(bt.at[h, zrow, q_cols(u, 1 - k)], fin.at[fin_rows(k, h), cols], sib))
            fin[fin_rows(k, h), cols] = bt[h, zrow, q_cols(u, k)]
    for copy in finals:
        copy.wait_recv()
    out[...] = fin[...].T
    for copy in started:
        copy.wait_send()

    for away, copy in a_sends:

        @pl.when(away)
        def _():
            copy.wait_send()


def local(projector, chol_vectors, screen_mask, amplitudes, pair_energy, rank_energy):
    a_own = amplitudes.reshape(2, 2, 64, 512)
    vmem = pl.BlockSpec(memory_space=pltpu.VMEM)
    back = pl.pallas_call(
        kernel,
        out_shape=jax.ShapeDtypeStruct((1024, 256), F32),
        in_specs=[pl.BlockSpec(memory_space=pltpu.SMEM), vmem, vmem, vmem],
        out_specs=vmem,
        scratch_shapes=[
            pltpu.VMEM((2, 2, 512, 1024), BF16),
            pltpu.VMEM((2, 256, 1024), BF16),
            pltpu.VMEM((2, 2, 4, 64, 1024), BF16),
            pltpu.VMEM((2, 2, 3, 64, 1024), BF16),
            pltpu.VMEM((2, 256, 2048), BF16),
            pltpu.VMEM((4, 2, 2, 512, 768), BF16),
            pltpu.VMEM((8, 4, 64, 768), BF16),
            pltpu.VMEM((8, 2, 32, 768), BF16),
            pltpu.VMEM((8, 2, 64, 768), BF16),
            pltpu.VMEM((2, 4, 256, 768), BF16),
            pltpu.VMEM((2, 256, 2048), F32),
            pltpu.VMEM((2, 4, 64, 2048), BF16),
            pltpu.VMEM((2, 3, 64, 2048), BF16),
            pltpu.VMEM((256, 1024), F32),
            pltpu.SemaphoreType.DMA((N_SEM,)),
            pltpu.SemaphoreType.DMA((N_SEM,)),
        ],
        compiler_params=pltpu.CompilerParams(
            collective_id=0, has_side_effects=True, vmem_limit_bytes=58 * 1024 * 1024
        ),
        cost_estimate=pl.CostEstimate(flops=16 * 10**9, bytes_accessed=8 * 10**6, transcendentals=0),
    )(screen_mask, projector, chol_vectors, a_own)
    return (back + projector.astype(F32)) / (pair_energy[:, None] + rank_energy[None, :])


def solution(mesh):
    placed = (
        P("pair", "chol"),
        P("pair", "chol"),
        P("pair", "chol"),
        P("chol", "pair"),
        P("pair"),
        P("chol"),
    )
    return jax.shard_map(local, mesh=mesh, in_specs=placed, out_specs=P("pair", "chol"), check_vma=False)
```

time: 166 us -> 143 us (0.86)
  Pallas kernels: 160 us -> 140 us
  local copies, waits for them, and re-layouts: 4.37 us -> 0.01 us
    pallas_call x1, Pallas kernels: 160 us -> 140 us  [local(): pl.pallas_call(kernel, out_shape=jax.ShapeDtypeStruct((1024, 256), F32),...]
    unnamed x6, local copies, waits for them, and re-layouts: 2.34 us -> 0.01 us
where the time goes in v2:
time: 143 us
  Pallas kernels  140 us (98%)
  other arithmetic  2.41 us (2%)
    pallas_call x1, Pallas kernels, local(): pl.pallas_call(kernel, out_shape=jax.ShapeDtypeStruct((1024, 256), F32),...  140 us

profile of v2, /device:TPU:1, one launch (start us, length us, event | category | flops | bytes accessed | tf_op | source)
XLA Modules:
  0.0 142.6 jit_solution(4882784838675933389)
XLA Ops:
  0.0 0.0 copy-start
  0.0 0.0 copy-start.1
  0.0 0.0 copy-start.2
  0.0 140.2 %shard_map.64 = f32[1024,256]{1,0:T(8,128)} custom-call(s32[8,6]{1,0:T(8,128)} %mask.1, bf16[1024,256]{1,0:T(8,128)(2,1)} %p_own.1, bf16[1024,768]{1,0:T(8,128)(2,1)} %s_own.1, bf16[2,2,64,512]{3,2,1,0:T(8,128)(2,1)} %bitcast.1), custom_call_target="tpu_custom_call" | custom-call | flops 16000000000 | bytes 8000000 | tf_op jit(solution)/shard_map/pallas_call | solution.py:324
  140.2 0.0 copy-done
  140.2 0.0 copy-done.1
  140.2 0.0 copy-done.2
  140.2 2.4 %add_divide_fusion = f32[1024,256]{1,0:T(8,128)} fusion(f32[1024,256]{1,0:T(8,128)} %shard_map.64, bf16[1024,256]{1,0:T(8,128)(2,1)S(1)} %copy-done, f32[256]{0:T(256)S(1)} %copy-done.2, f32[1024]{0:T(1024)S(1)} %copy-done.1), kind=kLoop, calls=%fused_computation | loop fusion | flops 1048576 | bytes 2626560 | tf_op jit(solution)/shard_map/div | solution.py:352
Async XLA Ops:
  0.0 140.2 %copy-start = (bf16[1024,256]{1,0:T(8,128)(2,1)S(1)}, bf16[1024,256]{1,0:T(8,128)(2,1)}, u32[]{:S(2)}) copy-start(bf16[1024,256]{1,0:T(8,128)(2,1)} %p_own.1) | copy-start | bytes 1572868
  0.0 140.2 %copy-start.1 = (f32[1024]{0:T(1024)S(1)}, f32[1024]{0:T(1024)}, u32[]{:S(2)}) copy-start(f32[1024]{0:T(1024)} %param.10) | copy-start | bytes 12292
  0.0 140.2 %copy-start.2 = (f32[256]{0:T(256)S(1)}, f32[256]{0:T(256)}, u32[]{:S(2)}) copy-start(f32[256]{0:T(256)} %param.11) | copy-start | bytes 3076

commit v3 on v2

--- a/solution.py
+++ b/solution.py
@@ -43,12 +43,6 @@
     friends = [sib, yl, yr, zl, zr, xl, xr_, at(dx=2), at(dy=2), at(dz=2)] + [at(dx=d, core=1 - k) for d in (1, 2, 3)]
     for friend in friends:
         pl.semaphore_signal(barrier, inc=1, device_id=friend, device_id_type=MESH)
-    for i in range(8):
-        u, rows = i // 4, slice(i % 4 * 128, i % 4 * 128 + 128)
-        for j in range(6):
-            keep = mask[i, j].astype(F32)
-            block = s_own[i * 128 : (i + 1) * 128, j * 128 : (j + 1) * 128].astype(F32) * keep
-            sg[0, u, k, rows, j * 128 : (j + 1) * 128] = block.astype(BF16)
     zcol = pl.ds(pl.multiple_of(z * 256, 256), 256)
     for u in range(2):
         pb[u, k, :, zcol] = p_own[u * 512 : (u + 1) * 512]
@@ -86,6 +80,12 @@
     p_ra = send(pb.at[1, k, a256, zcol], pb.at[1, k, a256, zcol], zr)
     p_lb = send(pb.at[1, k, b256, zcol], pb.at[1, k, b256, zcol], zl)
     p_sib = send(pb.at[:, k, :, zcol], pb.at[:, k, :, zcol], sib)
+    for i in range(8):
+        u, rows = i // 4, slice(i % 4 * 128, i % 4 * 128 + 128)
+        for j in range(6):
+            keep = mask[i, j].astype(F32)
+            block = s_own[i * 128 : (i + 1) * 128, j * 128 : (j + 1) * 128].astype(F32) * keep
+            sg[0, u, k, rows, j * 128 : (j + 1) * 128] = block.astype(BF16)
     lo, hi = slice(0, 384), slice(384, 768)
     s_r0 = [send(sg.at[0, u, k, :, lo], sg.at[1, u, k, :, hi], xr_) for u in range(2)]
     s_l0 = [send(sg.at[0, u, k, :, lo], sg.at[1, u, k, :, lo], xl) for u in range(2)]
@@ -261,21 +261,25 @@
         s["j"] = send(ref, ref, yl)
 
     done = [0, 0]
-    b_parts = [None, None]
+    b_parts = [[None, None], [None, None]]
 
     def stage4(t):
         h, g = TASKS[t]
         s = state[t]
         s["i"].wait_recv()
         s["j"].wait_recv()
-        part = lax.dot_general(tt[h, g], sg[g].reshape(2048, 768), (((1,), (1,)), ((), ())), preferred_element_type=F32)
-        if done[h]:
-            part += bt[h]
         done[h] += 1
-        bt[h] = part
-        if done[h] == 4:
-            bp[h] = part.astype(BF16).reshape(4, 64, 2048)
-            b_parts[h] = [send(bp.at[h, (z + d) % 4], br.at[h, d - 1], at(dz=d)) for d in (2, 1, 3)]
+        for u in range(2):
+            cols = slice(u * 1024, u * 1024 + 1024)
+            part = lax.dot_general(
+                tt[h, g], sg[g, u].reshape(1024, 768), (((1,), (1,)), ((), ())), preferred_element_type=F32
+            )
+            if done[h] > 1:
+                part += bt[h, :, cols]
+            bt[h, :, cols] = part
+            if done[h] == 4:
+                bp[h, u] = part.astype(BF16).reshape(4, 64, 1024)
+                b_parts[h][u] = [send(bp.at[h, u, (z + d) % 4], br.at[h, u, d - 1], at(dz=d)) for d in (2, 1, 3)]
 
     stages = (stage0, stage1, stage2, stage3, stage4)
     for tick in range(len(TASKS) + 4):
@@ -295,13 +299,14 @@
         return pl.ds(pl.multiple_of(core * 128 + h * 64, 64), 64)
 
     for h in range(2):
-        for copy in b_parts[h]:
-            copy.wait_recv()
-        total = bt[h, zrow, :]
-        for d in range(3):
-            total += br[h, d].astype(F32)
-        bt[h, zrow, :] = total
         for u in range(2):
+            cols = slice(u * 1024, u * 1024 + 1024)
+            for copy in b_parts[h][u]:
+                copy.wait_recv()
+            total = bt[h, zrow, cols]
+            for d in range(3):
+                total += br[h, u, d].astype(F32)
+            bt[h, zrow, cols] = total
             cols = slice(u * 512, u * 512 + 512)
             finals.append(send(bt.at[h, zrow, q_cols(u, 1 - k)], fin.at[fin_rows(k, h), cols], sib))
             fin[fin_rows(k, h), cols] = bt[h, zrow, q_cols(u, k)]
@@ -338,8 +343,8 @@
             pltpu.VMEM((8, 2, 64, 768), BF16),
             pltpu.VMEM((2, 4, 256, 768), BF16),
             pltpu.VMEM((2, 256, 2048), F32),
-            pltpu.VMEM((2, 4, 64, 2048), BF16),
-            pltpu.VMEM((2, 3, 64, 2048), BF16),
+            pltpu.VMEM((2, 2, 4, 64, 1024), BF16),
+            pltpu.VMEM((2, 2, 3, 64, 1024), BF16),
             pltpu.VMEM((256, 1024), F32),
             pltpu.SemaphoreType.DMA((N_SEM,)),
             pltpu.SemaphoreType.DMA((N_SEM,)),

time: 143 us -> 142 us (level)
  no operation moved by 1% of the time
where the time goes in v3:
time: 142 us
  Pallas kernels  140 us (99%)
  other arithmetic  2.41 us (2%)
    pallas_call x1, Pallas kernels, local(): pl.pallas_call(kernel, out_shape=jax.ShapeDtypeStruct((1024, 256), F32),...  140 us

profile of v3, /device:TPU:1, one launch (start us, length us, event | category | flops | bytes accessed | tf_op | source)
XLA Modules:
  0.0 142.0 jit_solution(2559687313609446777)
XLA Ops:
  0.0 0.0 copy-start
  0.0 0.0 copy-start.1
  0.0 0.0 copy-start.2
  0.0 139.6 %shard_map.64 = f32[1024,256]{1,0:T(8,128)} custom-call(s32[8,6]{1,0:T(8,128)} %mask.1, bf16[1024,256]{1,0:T(8,128)(2,1)} %p_own.1, bf16[1024,768]{1,0:T(8,128)(2,1)} %s_own.1, bf16[2,2,64,512]{3,2,1,0:T(8,128)(2,1)} %bitcast.1), custom_call_target="tpu_custom_call" | custom-call | flops 16000000000 | bytes 8000000 | tf_op jit(solution)/shard_map/pallas_call | solution.py:329
  139.6 0.0 copy-done
  139.6 0.0 copy-done.1
  139.6 0.0 copy-done.2
  139.6 2.4 %add_divide_fusion = f32[1024,256]{1,0:T(8,128)} fusion(f32[1024,256]{1,0:T(8,128)} %shard_map.64, bf16[1024,256]{1,0:T(8,128)(2,1)S(1)} %copy-done, f32[256]{0:T(256)S(1)} %copy-done.2, f32[1024]{0:T(1024)S(1)} %copy-done.1), kind=kLoop, calls=%fused_computation | loop fusion | flops 1048576 | bytes 2626560 | tf_op jit(solution)/shard_map/div | solution.py:357
Async XLA Ops:
  0.0 139.6 %copy-start = (bf16[1024,256]{1,0:T(8,128)(2,1)S(1)}, bf16[1024,256]{1,0:T(8,128)(2,1)}, u32[]{:S(2)}) copy-start(bf16[1024,256]{1,0:T(8,128)(2,1)} %p_own.1) | copy-start | bytes 1572868
  0.0 139.6 %copy-start.1 = (f32[1024]{0:T(1024)S(1)}, f32[1024]{0:T(1024)}, u32[]{:S(2)}) copy-start(f32[1024]{0:T(1024)} %param.10) | copy-start | bytes 12292
  0.0 139.6 %copy-start.2 = (f32[256]{0:T(256)S(1)}, f32[256]{0:T(256)}, u32[]{:S(2)}) copy-start(f32[256]{0:T(256)} %param.11) | copy-start | bytes 3076

commit v4 on v3

--- a/solution.py
+++ b/solution.py
@@ -202,7 +202,13 @@
         s_fl[u].wait_recv()
         s_shares[3].append(share(sg.at[3, u, k]))
 
-    after = {0: (lambda: x_sum(1, 1),), 2: (lambda: far(0),), 3: (lambda: far(1),), 5: (lambda: farther(0), lambda: farther(1))}
+    after = {
+        0: (lambda: x_sum(1, 1),),
+        1: (lambda: far(0),),
+        3: (lambda: far(1),),
+        4: (lambda: farther(0),),
+        5: (lambda: farther(1),),
+    }
 
     up, down, opp = (y + 1) % 4, (y + 3) % 4, (y + 2) % 4
     first, second = slice(0, 32), slice(32, 64)

time: 142 us -> 143 us (level)
  no operation moved by 1% of the time
where the time goes in v4:
time: 143 us; the launch traced here: 142 us
  Pallas kernels  140 us (98%)
  other arithmetic  2.41 us (2%)
    pallas_call x1, Pallas kernels, local(): pl.pallas_call(kernel, out_shape=jax.ShapeDtypeStruct((1024, 256), F32),...  140 us

profile of v4, /device:TPU:1, one launch (start us, length us, event | category | flops | bytes accessed | tf_op | source)
XLA Modules:
  0.0 142.0 jit_solution(4848973462423821345)
XLA Ops:
  0.0 0.0 copy-start
  0.0 0.0 copy-start.1
  0.0 0.0 copy-start.2
  0.0 139.6 %shard_map.64 = f32[1024,256]{1,0:T(8,128)} custom-call(s32[8,6]{1,0:T(8,128)} %mask.1, bf16[1024,256]{1,0:T(8,128)(2,1)} %p_own.1, bf16[1024,768]{1,0:T(8,128)(2,1)} %s_own.1, bf16[2,2,64,512]{3,2,1,0:T(8,128)(2,1)} %bitcast.1), custom_call_target="tpu_custom_call" | custom-call | flops 16000000000 | bytes 8000000 | tf_op jit(solution)/shard_map/pallas_call | solution.py:335
  139.6 0.0 copy-done
  139.6 0.0 copy-done.1
  139.6 0.0 copy-done.2
  139.6 2.4 %add_divide_fusion = f32[1024,256]{1,0:T(8,128)} fusion(f32[1024,256]{1,0:T(8,128)} %shard_map.64, bf16[1024,256]{1,0:T(8,128)(2,1)S(1)} %copy-done, f32[256]{0:T(256)S(1)} %copy-done.2, f32[1024]{0:T(1024)S(1)} %copy-done.1), kind=kLoop, calls=%fused_computation | loop fusion | flops 1048576 | bytes 2626560 | tf_op jit(solution)/shard_map/div | solution.py:363
Async XLA Ops:
  0.0 139.6 %copy-start = (bf16[1024,256]{1,0:T(8,128)(2,1)S(1)}, bf16[1024,256]{1,0:T(8,128)(2,1)}, u32[]{:S(2)}) copy-start(bf16[1024,256]{1,0:T(8,128)(2,1)} %p_own.1) | copy-start | bytes 1572868
  0.0 139.6 %copy-start.1 = (f32[1024]{0:T(1024)S(1)}, f32[1024]{0:T(1024)}, u32[]{:S(2)}) copy-start(f32[1024]{0:T(1024)} %param.10) | copy-start | bytes 12292
  0.0 139.6 %copy-start.2 = (f32[256]{0:T(256)S(1)}, f32[256]{0:T(256)}, u32[]{:S(2)}) copy-start(f32[256]{0:T(256)} %param.11) | copy-start | bytes 3076
